TPU v7x, 256 devices: a whole 4x4x8 slice. The times are simulated.
256 devices in a mesh: dp: 4 (over x), ep: 64 (over y, z, core).
Axes of the slice: x: 4, y: 4, z: 8, core: 2. Of those that a mesh axis runs over, the one named last changes fastest.
Arguments:
- tokens: bfloat16 [4, 2048, 2048], P('dp', 'ep'), may hold values from -12 to 12
- cotangent: bfloat16 [4, 2048, 2048], P('dp', 'ep'), may hold values from -6 to 6
- assign: int32 [4, 2048, 8], P('dp', 'ep'), may hold values from 0 to 63, as said below
- w_router: bfloat16 [2048, 64], replicated, may hold values from -0.125 to 0.125
- w_gate: bfloat16 [64, 2048, 768], P('ep'), may hold values from -0.125 to 0.125
- w_up: bfloat16 [64, 2048, 768], P('ep'), may hold values from -0.125 to 0.125
- w_down: bfloat16 [64, 2048, 768], P('ep'), may hold values from -0.21875 to 0.21875
Outputs:
- grad_tokens: bfloat16 [4, 2048, 2048], P('dp', 'ep')
- grad_router: float32 [2048, 64], replicated
- grad_gate: bfloat16 [64, 2048, 768], P('ep', 'dp')
- grad_up: bfloat16 [64, 2048, 768], P('ep', 'dp')
- grad_down: bfloat16 [64, 2048, 768], P('ep', 'dp')
Inputs may be any that keep to these rules, and one draw needn't show every extreme that they name: `assign`: each token names 8 different experts; the routes of the 32 tokens of one device name one expert at most 8 times, and in every draw one expert is named exactly 8 times by the routes of every device.
All inputs are finite; a program needn't handle non-finite values.
Results may differ from a plain program's by a relative error of at most 0.015.
Values may be sent and summed in bfloat16 or wider, within the bound.
A program may use at most 128 MiB of HBM per device.

v0:
```python
import jax
import jax.numpy as jnp
from jax import lax
from jax.sharding import PartitionSpec as P

ITERS = 3
cos_scale = 48.0
eps_norm = 1e-06
contract_first = (((0,), (0,)), ((), ()))
contract_last = (((1,), (1,)), ((), ()))


def logit_map(flat_tokens, router):
    inner_products = jnp.dot(flat_tokens, router, precision=lax.Precision.HIGHEST)
    token_norm = jnp.sqrt(jnp.sum(flat_tokens * flat_tokens, axis=1) + eps_norm)
    column_norm = jnp.sqrt(jnp.sum(router * router, axis=0) + eps_norm)
    return cos_scale * inner_products / (token_norm[:, None] * column_norm[None, :])


def expert_backward(expert_rows, expert_cotangent, rows_gate, gate_matrix, up_matrix, down_matrix):
    gate_linear = jnp.dot(expert_rows, gate_matrix, preferred_element_type=jnp.float32)
    up_linear = jnp.dot(expert_rows, up_matrix, preferred_element_type=jnp.float32)
    sigmoid_gate = jax.nn.sigmoid(gate_linear)
    activation = gate_linear * sigmoid_gate
    product = activation * up_linear
    hidden = product.astype(jnp.bfloat16)
    weighted = (rows_gate[:, None] * product).astype(jnp.bfloat16)
    raw_back = jnp.dot(expert_cotangent, down_matrix, preferred_element_type=jnp.float32)
    gate_grad = jnp.sum(raw_back * hidden.astype(jnp.float32), axis=1).astype(jnp.bfloat16)
    scaled_back = rows_gate[:, None] * raw_back
    up_delta = (scaled_back * activation).astype(jnp.bfloat16)
    gate_delta = (
        scaled_back * up_linear * sigmoid_gate * (1.0 + gate_linear * (1.0 - sigmoid_gate))
    ).astype(jnp.bfloat16)
    route_back = (
        lax.dot_general(gate_delta, gate_matrix, contract_last, preferred_element_type=jnp.float32)
        + lax.dot_general(up_delta, up_matrix, contract_last, preferred_element_type=jnp.float32)
    ).astype(jnp.bfloat16)
    return (gate_grad, route_back, gate_delta, up_delta, weighted)


def column_sums(values):
    return lax.psum(jnp.sum(values, axis=0), "ep")


def per_device(tokens, cotangent, assign, w_router, w_gate, w_up, w_down):
    local_tokens = tokens[0]
    local_cotangent = cotangent[0]
    route_ids = assign[0]
    token_count, per_token = route_ids.shape
    model_width = local_tokens.shape[1]
    experts = w_router.shape[1]
    slot_cap = min(token_count, 2 * token_count * per_token // experts)
    logits, logit_vjp = jax.vjp(
        logit_map, local_tokens.astype(jnp.float32), w_router.astype(jnp.float32)
    )
    kernel_start = jnp.exp(logits)
    kernel = kernel_start
    saved_steps = []
    for sweep_index in range(ITERS):
        column = column_sums(kernel)
        scaled = kernel / column[None, :]
        row_total = jnp.sum(scaled, axis=1, keepdims=True)
        kernel = scaled / row_total
        saved_steps.append((column, scaled, row_total, kernel))
    expert_ids = jnp.arange(experts, dtype=jnp.int32)
    onehot = (route_ids[:, :, None] == expert_ids).astype(jnp.float32)
    picked = jnp.sum(onehot * kernel[:, None, :], axis=2)
    picked_sum = jnp.sum(picked, axis=1, keepdims=True)
    gates = picked / picked_sum
    gate_half = gates.astype(jnp.bfloat16)
    flat_route = route_ids.reshape(-1)
    member = (flat_route[:, None] == expert_ids).astype(jnp.int32)
    earlier = jnp.cumsum(member, axis=0) - member
    slot_index = jnp.sum(earlier * member, axis=1)
    target = flat_route * slot_cap + slot_index
    route_slots = (
        jnp.arange(experts * slot_cap, dtype=jnp.int32)[:, None] == target[None, :]
    ).astype(jnp.bfloat16)
    token_slots = jnp.sum(route_slots.reshape(experts * slot_cap, token_count, per_token), axis=2)
    send_tokens = jnp.dot(token_slots, local_tokens, preferred_element_type=jnp.float32).astype(
        jnp.bfloat16
    )
    send_cotangent = jnp.dot(
        token_slots, local_cotangent, preferred_element_type=jnp.float32
    ).astype(jnp.bfloat16)
    send_gate = jnp.dot(
        route_slots, gate_half.reshape(-1), preferred_element_type=jnp.float32
    ).astype(jnp.bfloat16)
    recv_tokens, recv_cotangent, recv_gate = (
        lax.all_to_all(
            send_tokens.reshape(experts, slot_cap, model_width),
            "ep",
            split_axis=0,
            concat_axis=0,
            tiled=True,
        ),
        lax.all_to_all(
            send_cotangent.reshape(experts, slot_cap, model_width),
            "ep",
            split_axis=0,
            concat_axis=0,
            tiled=True,
        ),
        lax.all_to_all(
            send_gate.reshape(experts, slot_cap), "ep", split_axis=0, concat_axis=0, tiled=True
        ),
    )
    expert_rows = recv_tokens.reshape(-1, model_width)
    expert_cotangent = recv_cotangent.reshape(-1, model_width)
    rows_gate = recv_gate.reshape(-1).astype(jnp.float32)
    gate_grad, route_back, gate_delta, up_delta, weighted = expert_backward(
        expert_rows, expert_cotangent, rows_gate, w_gate[0], w_up[0], w_down[0]
    )
    back_rows, back_gate = (
        lax.all_to_all(
            route_back.reshape(experts, slot_cap, model_width),
            "ep",
            split_axis=0,
            concat_axis=0,
            tiled=True,
        ),
        lax.all_to_all(
            gate_grad.reshape(experts, slot_cap), "ep", split_axis=0, concat_axis=0, tiled=True
        ),
    )
    expert_back = lax.dot_general(
        token_slots,
        back_rows.reshape(-1, model_width),
        contract_first,
        preferred_element_type=jnp.float32,
    )
    route_grad = lax.dot_general(
        route_slots, back_gate.reshape(-1), contract_first, preferred_element_type=jnp.float32
    ).reshape(token_count, per_token)
    hidden_units = gate_delta.shape[1]
    summed = lax.psum_scatter(
        jnp.concatenate(
            [
                lax.dot_general(
                    expert_rows, gate_delta, contract_first, preferred_element_type=jnp.float32
                ),
                lax.dot_general(
                    expert_rows, up_delta, contract_first, preferred_element_type=jnp.float32
                ),
                lax.dot_general(
                    expert_cotangent, weighted, contract_first, preferred_element_type=jnp.float32
                ),
            ],
            axis=1,
        ).astype(jnp.bfloat16),
        "dp",
        scatter_dimension=0,
        tiled=True,
    ).astype(jnp.float32)
    grad_gate = summed[:, :hidden_units]
    grad_up = summed[:, hidden_units : 2 * hidden_units]
    grad_down = summed[:, 2 * hidden_units :]
    picked_grad = (route_grad - jnp.sum(route_grad * gates, axis=1, keepdims=True)) / picked_sum
    kernel_grad = jnp.sum(onehot * picked_grad[:, :, None], axis=1)
    for sweep_index in reversed(range(ITERS)):
        column, scaled, row_total, kernel_step = saved_steps[sweep_index]
        scaled_grad = (
            kernel_grad - jnp.sum(kernel_grad * kernel_step, axis=1, keepdims=True)
        ) / row_total
        moment = lax.psum(jnp.sum(scaled_grad * scaled, axis=0), "ep")
        kernel_grad = (scaled_grad - moment[None, :]) / column[None, :]
    logit_grad = kernel_grad * kernel_start
    router_back, router_part = logit_vjp(logit_grad)
    grad_router = lax.psum(router_part, ("dp", "ep"))
    grad_tokens = (expert_back + router_back).astype(jnp.bfloat16)[None]
    return (
        grad_tokens,
        grad_router,
        grad_gate.astype(jnp.bfloat16)[None],
        grad_up.astype(jnp.bfloat16)[None],
        grad_down.astype(jnp.bfloat16)[None],
    )


def solution(mesh):
    return jax.shard_map(
        per_device,
        mesh=mesh,
        in_specs=(
            P("dp", "ep", None),
            P("dp", "ep", None),
            P("dp", "ep", None),
            P(),
            P("ep", None, None),
            P("ep", None, None),
            P("ep", None, None),
        ),
        out_specs=(
            P("dp", "ep", None),
            P(),
            P("ep", "dp", None),
            P("ep", "dp", None),
            P("ep", "dp", None),
        ),
        check_vma=False,
    )
```

profile of v0, /device:TPU:2, one launch (start us, length us, event | category | flops | bytes accessed | tf_op | source)
XLA Modules:
  0.0 1251.3 jit_solution(17761611733418999477)
XLA Ops:
  10.0 1.1 fusion.32
  11.6 1.0 fusion.39
  13.3 1.8 fusion.76
  15.1 131.8 %psum.49 = f32[64]{0:T(128)S(1)} all-reduce(f32[64]{0:T(128)S(1)} %get-tuple-element.33), channel_id=1, replica_groups=mesh['dp'=4,'ep'=64] {'ep'}, use_global_device_ids=true, to_apply=%region_7.0 | all-reduce | flops 64 | bytes 512 | tf_op jit(solution)/shard_map/psum | solution.py:43
  147.1 124.1 %psum.50 = f32[64]{0:T(128)S(1)} all-reduce(f32[64]{0:T(128)S(1)} %fusion.67), channel_id=1, replica_groups=mesh['dp'=4,'ep'=64] {'ep'}, use_global_device_ids=true, to_apply=%region_10.0 | all-reduce | flops 64 | bytes 512 | tf_op jit(solution)/shard_map/psum | solution.py:43
  271.4 124.0 %psum.51 = f32[64]{0:T(128)S(1)} all-reduce(f32[64]{0:T(128)S(1)} %fusion.73), channel_id=1, replica_groups=mesh['dp'=4,'ep'=64] {'ep'}, use_global_device_ids=true, to_apply=%region_13.0 | all-reduce | flops 64 | bytes 512 | tf_op jit(solution)/shard_map/psum | solution.py:43
  398.9 4.6 all-to-all-start
  403.9 2.9 fusion.13
  406.9 6.1 all-to-all-done
  413.0 5.6 all-to-all-start.2
  418.6 2.1 fusion.12
  420.6 49.0 %all-to-all-done.2 = bf16[64,8,2048]{2,1,0:T(8,128)(2,1)} async-done(((bf16[64,8,2048]{2,1,0:T(8,128)(2,1)}), bf16[64,8,2048]{2,1,0:T(8,128)(2,1)}, u32[]{:S(2)}, u32[]{:S(2)}) %all-to-all-start.2) | async-done | bytes 2097184 | tf_op jit(solution)/shard_map/all_to_all | solution.py:91
  469.6 6.1 all-to-all-start.1
  476.1 5.5 fusion.6
  481.6 4.6 fusion.2
  486.2 40.5 %all-to-all-done.1 = bf16[64,8,2048]{2,1,0:T(8,128)(2,1)} async-done(((bf16[64,8,2048]{2,1,0:T(8,128)(2,1)}), bf16[64,8,2048]{2,1,0:T(8,128)(2,1)}, u32[]{:S(2)}, u32[]{:S(2)}) %all-to-all-start.1) | async-done | bytes 2097184 | tf_op jit(solution)/shard_map/all_to_all | solution.py:98
  526.7 4.6 convolution_convert_fusion
  531.4 4.0 multiply_reduce_fusion
  535.4 4.0 convolution_convert_fusion.1
  539.5 3.4 convolution_convert_fusion.2
  542.9 4.5 pad_maximum_fusion
  548.1 6.4 all-to-all-start.4
  554.5 3.3 fusion
  557.8 3.1 fusion.14
  560.9 2.6 all-to-all-done.4
  563.5 7.7 all-to-all-start.3
  571.3 1.5 reduce.4
  572.7 1.4 reshape.169
  574.1 1.4 fusion.37
  575.6 0.9 multiply_reduce_fusion.9
  579.5 1.3 multiply_reduce_fusion.7
  580.8 155.9 %psum.52 = f32[64]{0:T(128)} all-reduce(f32[64]{0:T(128)} %multiply_reduce_fusion.7), channel_id=1, replica_groups=mesh['dp'=4,'ep'=64] {'ep'}, use_global_device_ids=true, to_apply=%region_22.23 | all-reduce | flops 64 | bytes 512 | tf_op jit(solution)/shard_map/psum | solution.py:166
  736.7 0.9 multiply_reduce_fusion.6
  737.7 2.0 multiply_reduce_fusion.5
  739.6 124.5 %psum.53 = f32[64]{0:T(128)} all-reduce(f32[64]{0:T(128)} %get-tuple-element.31), channel_id=1, replica_groups=mesh['dp'=4,'ep'=64] {'ep'}, use_global_device_ids=true, to_apply=%region_25.26 | all-reduce | flops 64 | bytes 512 | tf_op jit(solution)/shard_map/psum | solution.py:166
  865.6 1.3 multiply_reduce_fusion.3
  866.9 124.7 %psum.54 = f32[64]{0:T(128)} all-reduce(f32[64]{0:T(128)} %multiply_reduce_fusion.3), channel_id=1, replica_groups=mesh['dp'=4,'ep'=64] {'ep'}, use_global_device_ids=true, to_apply=%region_28.29 | all-reduce | flops 64 | bytes 512 | tf_op jit(solution)/shard_map/psum | solution.py:166
  992.5 1.3 multiply_reduce_fusion.1
  994.5 1.9 fusion.17
  996.4 1.2 multiply_multiply_fusion.3
  997.6 2.1 fusion.21
  999.7 1.0 fusion.20
  1000.8 3.1 slice_bitcast_fusion
  1003.8 2.3 copy.39
  1006.1 2.3 copy.40
  1008.4 2.3 copy.41
  1010.7 231.3 %all-reduce.2.cloned.1.call-done = f32[2048,64]{0,1:T(8,128)} async-done(((f32[2048,64]{0,1:T(8,128)}), f32[2048,64]{0,1:T(8,128)}) %all-reduce.2.cloned.1.call-update) | async-done | bytes 524304 | tf_op jit(solution)/shard_map/psum | solution.py:170
  1242.0 1.9 copy.46
  (110 shorter events, 14.5 us)
Async XLA Ops:
  8.0 473.6 %copy-start = (bf16[1,2048,768]{2,1,0:T(8,128)(2,1)S(1)}, bf16[1,2048,768]{2,1,0:T(8,128)(2,1)}, u32[]{:S(2)}) copy-start(bf16[1,2048,768]{2,1,0:T(8,128)(2,1)} %param.11) | copy-start | bytes 9437188
  8.9 404.0 %copy-start.3 = (s32[1,32,8]{2,1,0:T(8,128)}, s32[1,32,8]{2,1,0:T(8,128)S(1)}, u32[]{:S(2)}) copy-start(s32[1,32,8]{2,1,0:T(8,128)S(1)} %copy.33) | copy-start | bytes 3076
  11.1 0.6 copy-start.25
  11.6 3.5 copy-start.16
  12.7 0.6 copy-start.24
  13.3 1.8 copy-start.18
  146.9 257.0 %copy-start.10 = (f32[64]{0:T(128)}, f32[64]{0:T(128)S(1)}, u32[]{:S(2)}) copy-start(f32[64]{0:T(128)S(1)} %psum.49) | copy-start | bytes 772
  147.0 256.9 %copy-start.11 = (f32[32]{0:T(128)}, f32[32]{0:T(128)S(1)}, u32[]{:S(2)}) copy-start(f32[32]{0:T(128)S(1)} %fusion.65) | copy-start | bytes 388
  271.2 132.7 %copy-start.12 = (f32[64]{0:T(128)}, f32[64]{0:T(128)S(1)}, u32[]{:S(2)}) copy-start(f32[64]{0:T(128)S(1)} %psum.50) | copy-start | bytes 772
  271.3 132.6 %copy-start.13 = (f32[32]{0:T(128)}, f32[32]{0:T(128)S(1)}, u32[]{:S(2)}) copy-start(f32[32]{0:T(128)S(1)} %fusion.70) | copy-start | bytes 388
  395.5 1.3 copy-start.14
  395.7 0.5 copy-start.15
  396.7 0.6 copy-start.8
  396.8 7.2 copy-start.21
  397.6 0.6 copy-start.23
  398.9 14.0 %all-to-all-start = ((bf16[64,1,8]{2,1,0:T(2,128)(2,1)}), bf16[64,1,8]{2,1,0:T(2,128)(2,1)S(1)}, u32[]{:S(2)}, u32[]{:S(2)}) async-start(bf16[64,1,8]{2,1,0:T(2,128)(2,1)} %all_to_all.25), calls=%async_computation | async-start | bytes 65536 | tf_op jit(solution)/shard_map/all_to_all | solution.py:105
  403.9 14.6 %copy-start.4 = (bf16[512,32]{0,1:T(8,128)(2,1)}, bf16[512,32]{0,1:T(8,128)(2,1)S(1)}, u32[]{:S(2)}) copy-start(bf16[512,32]{0,1:T(8,128)(2,1)S(1)} %fusion.41) | copy-start | bytes 98308
  406.9 11.7 copy-start.9
  413.0 56.6 %all-to-all-start.2 = ((bf16[64,8,2048]{2,1,0:T(8,128)(2,1)}), bf16[64,8,2048]{2,1,0:T(8,128)(2,1)}, u32[]{:S(2)}, u32[]{:S(2)}) async-start(bf16[64,8,2048]{2,1,0:T(8,128)(2,1)} %fusion.13), calls=%async_computation.2 | async-start | bytes 4194304 | tf_op jit(solution)/shard_map/all_to_all | solution.py:91
  469.6 57.2 %all-to-all-start.1 = ((bf16[64,8,2048]{2,1,0:T(8,128)(2,1)}), bf16[64,8,2048]{2,1,0:T(8,128)(2,1)}, u32[]{:S(2)}, u32[]{:S(2)}) async-start(bf16[64,8,2048]{2,1,0:T(8,128)(2,1)} %fusion.12), calls=%async_computation.1 | async-start | bytes 4194304 | tf_op jit(solution)/shard_map/all_to_all | solution.py:98
  475.7 525.0 %reduce-scatter.2.cloned.1.call-start = ((), (), s32[]{:S(2)}) async-start(), calls=%async_computation.7 | async-start | bytes 11796480 | tf_op jit(solution)/shard_map/reduce_scatter | solution.py:137
  526.7 4.6 copy-start.27
  526.7 4.7 copy-start.32
  526.7 4.7 copy-start.33
  535.4 4.0 copy-start.29
  535.4 4.0 copy-start.31
  548.1 15.4 %all-to-all-start.4 = ((bf16[64,1,8]{2,1,0:T(2,128)(2,1)}), bf16[64,1,8]{2,1,0:T(2,128)(2,1)}, u32[]{:S(2)}, u32[]{:S(2)}) async-start(bf16[64,1,8]{2,1,0:T(2,128)(2,1)} %convert_element_type.108), calls=%async_computation.4 | async-start | bytes 65536 | tf_op jit(solution)/shard_map/all_to_all | solution.py:123
  554.5 3.3 copy-start.28
  554.5 3.3 copy-start.30
  560.9 433.5 %copy-start.1 = (bf16[2048,64]{0,1:T(8,128)(2,1)S(1)}, bf16[2048,64]{0,1:T(8,128)(2,1)}, u32[]{:S(2)}) copy-start(bf16[2048,64]{0,1:T(8,128)(2,1)} %param.10) | copy-start | bytes 786436
  560.9 433.5 %copy-start.2 = (bf16[1,32,2048]{2,1,0:T(8,128)(2,1)S(1)}, bf16[1,32,2048]{2,1,0:T(8,128)(2,1)}, u32[]{:S(2)}) copy-start(bf16[1,32,2048]{2,1,0:T(8,128)(2,1)} %param.7) | copy-start | bytes 393220
  563.5 434.1 %all-to-all-start.3 = ((bf16[64,8,2048]{2,1,0:T(8,128)(2,1)}), bf16[64,8,2048]{2,1,0:T(8,128)(2,1)}, u32[]{:S(2)}, u32[]{:S(2)}) async-start(bf16[64,8,2048]{2,1,0:T(8,128)(2,1)} %fusion.14), calls=%async_computation.3 | async-start | bytes 4194304 | tf_op jit(solution)/shard_map/all_to_all | solution.py:116
  571.2 670.8 %all-reduce.2.cloned.1.call-start = ((), (), s32[]{:S(2)}) async-start(), calls=%async_computation.6 | async-start | bytes 1048576 | tf_op jit(solution)/shard_map/psum | solution.py:170
  578.1 0.9 copy-start.5
  579.0 0.5 copy-start.20
  865.1 0.5 copy-start.22
  992.5 2.0 copy-start.6
  996.4 3.3 copy-start.7
  997.6 2.1 copy-start.17
  997.6 2.1 copy-start.19
  997.6 2.1 copy-start.26
Sparse Core Ops, SparseCore 0:
  547.5 87.0 reduce-scatter.1
Sparse Core Ops, SparseCore 1:
  996.5 245.4 all-reduce.1
where the time goes:
time: 1250 us
  blocking collectives  785 us (63%)
  waiting for transfers between devices  330 us (26%)
  matrix products  46 us (4%)
  starting transfers between devices  30.6 us (2%)
  other arithmetic  24.4 us (2%)
  local copies, waits for them, and re-layouts  19.8 us (2%)
  between operations  16 us (1%)
    psum x3, blocking collectives, per_device(): moment = lax.psum(jnp.sum(scaled_grad * scaled, axis=0), 'ep')  405 us
    psum x3, blocking collectives, column_sums(): return lax.psum(jnp.sum(values, axis=0), 'ep')  380 us
    psum x1, waiting for transfers between devices, per_device(): grad_router = lax.psum(router_part, ('dp', 'ep'))  231 us
    all_to_all x1, waiting for transfers between devices, per_device(): lax.all_to_all(send_tokens.reshape(experts, slot_cap, model_width), 'ep',...  49 us
    all_to_all x1, waiting for transfers between devices, per_device(): lax.all_to_all(send_cotangent.reshape(experts, slot_cap, model_width), 'e...  40.5 us
  transfers between devices with their start and end apart: 7, of which 5 were waited for; matrix products, arithmetic and copies ran while one was open for 4% of the time, Pallas kernels for 0%

commit v1 on v0

--- a/solution.py
+++ b/solution.py
@@ -167,7 +167,7 @@
         kernel_grad = (scaled_grad - moment[None, :]) / column[None, :]
     logit_grad = kernel_grad * kernel_start
     router_back, router_part = logit_vjp(logit_grad)
-    grad_router = lax.psum(router_part, ("dp", "ep"))
+    grad_router = lax.psum(lax.psum(router_part, axis_name="ep"), axis_name="dp")
     grad_tokens = (expert_back + router_back).astype(jnp.bfloat16)[None]
     return (
         grad_tokens,

time: 1250 us -> 1200 us (0.960)
  waiting for transfers between devices: 330 us -> 293 us
  blocking collectives: 785 us -> 758 us
    psum x1 -> x2, waiting for transfers between devices: 231 us -> 197 us  [the longest x1 166 us: per_device(): lax.psum(router_part, axis_name='ep')]
    psum x3, blocking collectives: 405 us -> 378 us  [per_device(): moment = lax.psum(jnp.sum(scaled_grad * scaled, axis=0), 'ep')]
  transfers between devices with their start and end apart: 7 -> 8, of which waited for: 5 -> 5; matrix products, arithmetic and copies ran while one was open for 4% -> 5% of each run, Pallas kernels for 0% -> 0%
where the time goes in v1:
time: 1200 us
  blocking collectives  758 us (63%)
  waiting for transfers between devices  293 us (24%)
  matrix products  53.2 us (4%)
  starting transfers between devices  28.1 us (2%)
  other arithmetic  27.6 us (2%)
  local copies, waits for them, and re-layouts  19.2 us (2%)
  between operations  16 us (1%)
    psum x3, blocking collectives, column_sums(): return lax.psum(jnp.sum(values, axis=0), 'ep')  380 us
    psum x3, blocking collectives, per_device(): moment = lax.psum(jnp.sum(scaled_grad * scaled, axis=0), 'ep')  378 us
    psum x1, waiting for transfers between devices, per_device(): lax.psum(router_part, axis_name='ep')  166 us
    all_to_all x1, waiting for transfers between devices, per_device(): lax.all_to_all(send_tokens.reshape(experts, slot_cap, model_width), 'ep',...  49 us
    all_to_all x1, waiting for transfers between devices, per_device(): lax.all_to_all(send_cotangent.reshape(experts, slot_cap, model_width), 'e...  40.8 us
    psum x1, waiting for transfers between devices, per_device(): lax.psum(lax.psum(router_part, axis_name='ep'), axis_name='dp')  31.4 us
  transfers between devices with their start and end apart: 8, of which 5 were waited for; matrix products, arithmetic and copies ran while one was open for 5% of the time, Pallas kernels for 0%

profile of v1, /device:TPU:2, one launch (start us, length us, event | category | flops | bytes accessed | tf_op | source)
XLA Modules:
  0.0 1195.3 jit_solution(728975241598417634)
XLA Ops:
  10.0 1.1 fusion.32
  11.6 1.0 fusion.39
  12.7 1.8 fusion.76
  14.5 131.8 %psum.56 = f32[64]{0:T(128)S(1)} all-reduce(f32[64]{0:T(128)S(1)} %get-tuple-element.33), channel_id=1, replica_groups=mesh['dp'=4,'ep'=64] {'ep'}, use_global_device_ids=true, to_apply=%region_7.0 | all-reduce | flops 64 | bytes 512 | tf_op jit(solution)/shard_map/psum | solution.py:43
  146.5 124.1 %psum.57 = f32[64]{0:T(128)S(1)} all-reduce(f32[64]{0:T(128)S(1)} %fusion.67), channel_id=1, replica_groups=mesh['dp'=4,'ep'=64] {'ep'}, use_global_device_ids=true, to_apply=%region_10.0 | all-reduce | flops 64 | bytes 512 | tf_op jit(solution)/shard_map/psum | solution.py:43
  270.9 124.0 %psum.58 = f32[64]{0:T(128)S(1)} all-reduce(f32[64]{0:T(128)S(1)} %fusion.73), channel_id=1, replica_groups=mesh['dp'=4,'ep'=64] {'ep'}, use_global_device_ids=true, to_apply=%region_13.0 | all-reduce | flops 64 | bytes 512 | tf_op jit(solution)/shard_map/psum | solution.py:43
  398.3 4.6 all-to-all-start
  403.3 2.9 fusion.13
  406.3 6.1 all-to-all-done
  412.4 5.6 all-to-all-start.2
  417.9 2.1 fusion.12
  420.0 49.0 %all-to-all-done.2 = bf16[64,8,2048]{2,1,0:T(8,128)(2,1)} async-done(((bf16[64,8,2048]{2,1,0:T(8,128)(2,1)}), bf16[64,8,2048]{2,1,0:T(8,128)(2,1)}, u32[]{:S(2)}, u32[]{:S(2)}) %all-to-all-start.2) | async-done | bytes 2097184 | tf_op jit(solution)/shard_map/all_to_all | solution.py:91
  468.9 6.1 all-to-all-start.1
  475.3 5.5 fusion.6
  480.7 4.6 fusion.2
  485.4 40.8 %all-to-all-done.1 = bf16[64,8,2048]{2,1,0:T(8,128)(2,1)} async-done(((bf16[64,8,2048]{2,1,0:T(8,128)(2,1)}), bf16[64,8,2048]{2,1,0:T(8,128)(2,1)}, u32[]{:S(2)}, u32[]{:S(2)}) %all-to-all-start.1) | async-done | bytes 2097184 | tf_op jit(solution)/shard_map/all_to_all | solution.py:98
  526.1 6.9 multiply_reduce_fusion
  533.7 6.1 all-to-all-start.4
  539.9 6.2 convolution_convert_fusion
  546.1 5.2 convolution_convert_fusion.1
  551.3 5.2 convolution_convert_fusion.2
  556.5 1.5 reduce.4
  557.9 1.4 reshape.169
  559.3 1.4 fusion.37
  560.8 0.9 multiply_reduce_fusion.9
  564.8 1.3 multiply_reduce_fusion.7
  566.0 129.4 %psum.59 = f32[64]{0:T(128)} all-reduce(f32[64]{0:T(128)} %multiply_reduce_fusion.7), channel_id=1, replica_groups=mesh['dp'=4,'ep'=64] {'ep'}, use_global_device_ids=true, to_apply=%region_22.23 | all-reduce | flops 64 | bytes 512 | tf_op jit(solution)/shard_map/psum | solution.py:166
  695.4 0.9 multiply_reduce_fusion.6
  696.3 2.0 multiply_reduce_fusion.5
  698.3 124.6 %psum.60 = f32[64]{0:T(128)} all-reduce(f32[64]{0:T(128)} %get-tuple-element.31), channel_id=1, replica_groups=mesh['dp'=4,'ep'=64] {'ep'}, use_global_device_ids=true, to_apply=%region_25.26 | all-reduce | flops 64 | bytes 512 | tf_op jit(solution)/shard_map/psum | solution.py:166
  824.3 1.3 multiply_reduce_fusion.3
  825.6 124.5 %psum.61 = f32[64]{0:T(128)} all-reduce(f32[64]{0:T(128)} %multiply_reduce_fusion.3), channel_id=1, replica_groups=mesh['dp'=4,'ep'=64] {'ep'}, use_global_device_ids=true, to_apply=%region_28.29 | all-reduce | flops 64 | bytes 512 | tf_op jit(solution)/shard_map/psum | solution.py:166
  951.0 1.4 multiply_reduce_fusion.1
  953.0 2.0 fusion.17
  955.0 7.7 pad_maximum_fusion
  962.8 3.1 fusion
  965.9 3.1 fusion.14
  969.0 5.6 all-to-all-start.3
  974.7 1.2 multiply_multiply_fusion.3
  975.8 165.6 %all-reduce.3.cloned.1.call-done = f32[2048,64]{0,1:T(8,128)} async-done(((f32[2048,64]{0,1:T(8,128)}), f32[2048,64]{0,1:T(8,128)}) %all-reduce.3.cloned.1.call-update) | async-done | bytes 524304 | tf_op jit(solution)/shard_map/psum | solution.py:170
  1141.5 2.1 fusion.21
  1143.6 1.0 fusion.20
  1144.6 3.1 slice_bitcast_fusion
  1147.7 2.3 copy.39
  1150.0 2.3 copy.40
  1152.3 2.3 copy.41
  1154.6 31.4 %all-reduce.5.cloned.1.call-done = f32[2048,64]{0,1:T(8,128)} async-done(((f32[2048,64]{0,1:T(8,128)}), f32[2048,64]{0,1:T(8,128)}) %all-reduce.5.cloned.1.call-update) | async-done | bytes 524304 | tf_op jit(solution)/shard_map/psum | solution.py:170
  1186.0 1.9 copy.47
  (107 shorter events, 13.7 us)
Async XLA Ops:
  8.0 472.7 %copy-start = (bf16[1,2048,768]{2,1,0:T(8,128)(2,1)S(1)}, bf16[1,2048,768]{2,1,0:T(8,128)(2,1)}, u32[]{:S(2)}) copy-start(bf16[1,2048,768]{2,1,0:T(8,128)(2,1)} %param.11) | copy-start | bytes 9437188
  8.9 403.4 %copy-start.3 = (s32[1,32,8]{2,1,0:T(8,128)}, s32[1,32,8]{2,1,0:T(8,128)S(1)}, u32[]{:S(2)}) copy-start(s32[1,32,8]{2,1,0:T(8,128)S(1)} %copy.33) | copy-start | bytes 3076
  11.1 0.5 copy-start.25
  11.6 2.9 copy-start.16
  12.7 1.9 copy-start.24
  12.7 1.9 copy-start.18
  146.3 256.9 %copy-start.10 = (f32[64]{0:T(128)}, f32[64]{0:T(128)S(1)}, u32[]{:S(2)}) copy-start(f32[64]{0:T(128)S(1)} %psum.56) | copy-start | bytes 772
  146.4 256.8 %copy-start.11 = (f32[32]{0:T(128)}, f32[32]{0:T(128)S(1)}, u32[]{:S(2)}) copy-start(f32[32]{0:T(128)S(1)} %fusion.65) | copy-start | bytes 388
  270.6 132.7 %copy-start.12 = (f32[64]{0:T(128)}, f32[64]{0:T(128)S(1)}, u32[]{:S(2)}) copy-start(f32[64]{0:T(128)S(1)} %psum.57) | copy-start | bytes 772
  270.8 132.5 %copy-start.13 = (f32[32]{0:T(128)}, f32[32]{0:T(128)S(1)}, u32[]{:S(2)}) copy-start(f32[32]{0:T(128)S(1)} %fusion.70) | copy-start | bytes 388
  394.9 1.3 copy-start.14
  395.1 0.5 copy-start.15
  396.2 0.6 copy-start.8
  396.2 7.1 copy-start.21
  397.1 0.5 copy-start.23
  398.3 14.0 %all-to-all-start = ((bf16[64,1,8]{2,1,0:T(2,128)(2,1)}), bf16[64,1,8]{2,1,0:T(2,128)(2,1)S(1)}, u32[]{:S(2)}, u32[]{:S(2)}) async-start(bf16[64,1,8]{2,1,0:T(2,128)(2,1)} %all_to_all.25), calls=%async_computation | async-start | bytes 65536 | tf_op jit(solution)/shard_map/all_to_all | solution.py:105
  403.3 14.6 %copy-start.4 = (bf16[512,32]{0,1:T(8,128)(2,1)}, bf16[512,32]{0,1:T(8,128)(2,1)S(1)}, u32[]{:S(2)}) copy-start(bf16[512,32]{0,1:T(8,128)(2,1)S(1)} %fusion.41) | copy-start | bytes 98308
  406.3 11.7 copy-start.9
  412.4 56.6 %all-to-all-start.2 = ((bf16[64,8,2048]{2,1,0:T(8,128)(2,1)}), bf16[64,8,2048]{2,1,0:T(8,128)(2,1)}, u32[]{:S(2)}, u32[]{:S(2)}) async-start(bf16[64,8,2048]{2,1,0:T(8,128)(2,1)} %fusion.13), calls=%async_computation.2 | async-start | bytes 4194304 | tf_op jit(solution)/shard_map/all_to_all | solution.py:91
  468.9 57.2 %all-to-all-start.1 = ((bf16[64,8,2048]{2,1,0:T(8,128)(2,1)}), bf16[64,8,2048]{2,1,0:T(8,128)(2,1)}, u32[]{:S(2)}, u32[]{:S(2)}) async-start(bf16[64,8,2048]{2,1,0:T(8,128)(2,1)} %fusion.12), calls=%async_computation.1 | async-start | bytes 4194304 | tf_op jit(solution)/shard_map/all_to_all | solution.py:98
  533.7 22.8 %all-to-all-start.4 = ((bf16[64,1,8]{2,1,0:T(2,128)(2,1)}), bf16[64,1,8]{2,1,0:T(2,128)(2,1)}, u32[]{:S(2)}, u32[]{:S(2)}) async-start(bf16[64,1,8]{2,1,0:T(2,128)(2,1)} %convert_element_type.108), calls=%async_computation.4 | async-start | bytes 65536 | tf_op jit(solution)/shard_map/all_to_all | solution.py:123
  539.9 601.6 %all-reduce.3.cloned.1.call-start = ((), (), s32[]{:S(2)}) async-start(), calls=%async_computation.6 | async-start | bytes 1048576 | tf_op jit(solution)/shard_map/psum | solution.py:170
  539.9 6.2 copy-start.28
  546.1 5.2 copy-start.30
  551.3 401.7 %copy-start.1 = (bf16[2048,64]{0,1:T(8,128)(2,1)S(1)}, bf16[2048,64]{0,1:T(8,128)(2,1)}, u32[]{:S(2)}) copy-start(bf16[2048,64]{0,1:T(8,128)(2,1)} %param.10) | copy-start | bytes 786436
  551.3 401.7 %copy-start.2 = (bf16[1,32,2048]{2,1,0:T(8,128)(2,1)S(1)}, bf16[1,32,2048]{2,1,0:T(8,128)(2,1)}, u32[]{:S(2)}) copy-start(bf16[1,32,2048]{2,1,0:T(8,128)(2,1)} %param.7) | copy-start | bytes 393220
  563.3 0.9 copy-start.5
  564.2 0.5 copy-start.20
  823.8 0.5 copy-start.22
  951.0 2.0 copy-start.6
  955.0 189.7 %reduce-scatter.2.cloned.1.call-start = ((), (), s32[]{:S(2)}) async-start(), calls=%async_computation.8 | async-start | bytes 11796480 | tf_op jit(solution)/shard_map/reduce_scatter | solution.py:137
  962.7 3.1 copy-start.27
  962.7 3.1 copy-start.29
  969.0 172.5 %all-to-all-start.3 = ((bf16[64,8,2048]{2,1,0:T(8,128)(2,1)}), bf16[64,8,2048]{2,1,0:T(8,128)(2,1)}, u32[]{:S(2)}, u32[]{:S(2)}) async-start(bf16[64,8,2048]{2,1,0:T(8,128)(2,1)} %fusion.14), calls=%async_computation.3 | async-start | bytes 4194304 | tf_op jit(solution)/shard_map/all_to_all | solution.py:116
  974.6 169.0 %copy-start.7 = (f32[32,64]{1,0:T(8,128)S(1)}, f32[32,64]{1,0:T(8,128)}, u32[]{:S(2)}) copy-start(f32[32,64]{1,0:T(8,128)} %copy-done.6) | copy-start | bytes 24580
  974.6 211.4 %all-reduce.5.cloned.1.call-start = ((), (), s32[]{:S(2)}) async-start(), calls=%async_computation.7 | async-start | bytes 1048576 | tf_op jit(solution)/shard_map/psum | solution.py:170
  1141.5 2.1 copy-start.17
  1141.5 2.1 copy-start.19
  1141.5 2.1 copy-start.26
Sparse Core Ops, SparseCore 0:
  955.1 186.3 all-reduce.2
Sparse Core Ops, SparseCore 1:
  962.8 83.9 reduce-scatter.1
  1141.6 44.4 all-reduce.4
